TPU v7x, 32 devices: a whole 2x2x4 slice. The times are simulated.
32 devices in a mesh: slab: 4 (over y, x), expert: 8 (over z, core).
Axes of the slice: x: 2, y: 2, z: 4, core: 2. Of those that a mesh axis runs over, the one named last changes fastest.
Arguments:
- features: bfloat16 [8, 32, 64, 1024], P('expert', 'slab'), may hold values from -6 to 6
- expert_ids: int32 [8, 32, 64, 2], P('expert', 'slab'), may hold values from 0 to 7, as said below
- positions: int32 [8, 32, 64, 2], P('expert', 'slab'), may hold values from 0 to 511, as said below
- gates: float32 [8, 32, 64, 2], P('expert', 'slab'), may hold values from 0.2 to 1
- w_in: bfloat16 [8, 1024, 4096], P('expert'), may hold values from -0.1875 to 0.1875
- w_out: bfloat16 [8, 4096, 1024], P('expert'), may hold values from -0.09375 to 0.09375
- w_proj: bfloat16 [1024, 256], replicated, may hold values from -0.1875 to 0.1875
- kernel_one: bfloat16 [3, 3, 256, 256], replicated, may hold values from -0.125 to 0.125
- kernel_two: bfloat16 [3, 3, 256, 256], replicated, may hold values from -0.125 to 0.125
Outputs:
- joined: bfloat16 [8, 32, 64, 256], P('expert', 'slab')
Inputs may be any that keep to these rules, and one draw needn't show every extreme that they name: `expert_ids`: the two experts of a token differ. Within one band, the assignments to one expert hold the positions 0, 1, 2, ... each once.
All inputs are finite; a program needn't handle non-finite values.
Results may differ from a plain program's by a relative error of at most 0.009.
Values may be sent and summed in bfloat16 or wider, within the bound.
A program may use at most 128 MiB of HBM per device.

v0:
```python
import jax
import jax.numpy as jnp
from jax import lax
from jax.sharding import PartitionSpec as P


def padded_2(block, sides, width):
    for axis, dim in sides:
        count = lax.axis_size(axis)
        forward = [(i, i + 1) for i in range(count - 1)]
        backward = [(target, source) for source, target in forward]
        low = lax.ppermute(
            lax.slice_in_dim(block, block.shape[dim] - width, None, axis=dim), axis, forward
        )
        high = lax.ppermute(lax.slice_in_dim(block, 0, width, axis=dim), axis, backward)
        block = jnp.concatenate([low, block, high], axis=dim)
    return block


def conv_rows(padded, kernel):
    out_rows = padded.shape[0] - 2
    width_cols = padded.shape[1]
    channels = padded.shape[2]
    widened = jnp.pad(padded, ((0, 0), (1, 1), (0, 0)))
    columns = jnp.concatenate(
        [widened[:, 0:width_cols], widened[:, 1 : width_cols + 1], widened[:, 2 : width_cols + 2]],
        axis=-1,
    )
    kernel_taps = kernel.reshape(3, 3 * channels, -1)
    total = jnp.zeros((out_rows * width_cols, kernel.shape[3]), jnp.float32)
    for row_shift in range(3):
        window = columns[row_shift : row_shift + out_rows].reshape(
            out_rows * width_cols, 3 * channels
        )
        total = total + jnp.dot(window, kernel_taps[row_shift], preferred_element_type=jnp.float32)
    return total.reshape(out_rows, width_cols, -1)


def shards(features, expert_ids, positions, gates, w_in, w_out, w_proj, kernel_one, kernel_two):
    maps_dev, rows_dev, width_cols, model_width = features.shape
    tokens_dev = rows_dev * width_cols
    owners = lax.axis_size("expert")
    local_experts = w_in.shape[0]
    experts_all = owners * local_experts
    capacity = 3 * tokens_dev // experts_all
    resident = features.reshape(tokens_dev, model_width)
    wide32 = resident.astype(jnp.float32)
    normed = (wide32 * lax.rsqrt(jnp.mean(wide32 * wide32, axis=1, keepdims=True) + 1e-06)).astype(
        jnp.bfloat16
    )
    slot_ids = expert_ids.reshape(-1)
    slot_pos = positions.reshape(-1)
    usable = slot_pos < capacity
    slot_index = jnp.where(usable, slot_ids * capacity + slot_pos, experts_all * capacity)
    token_rows = jnp.repeat(normed, 2, axis=0)
    buffer = jnp.zeros((experts_all * capacity, model_width), jnp.bfloat16)
    buffer = (
        buffer.at[slot_index]
        .set(token_rows, mode="drop")
        .reshape(experts_all, capacity, model_width)
    )
    received = lax.all_to_all(buffer, "expert", split_axis=0, concat_axis=0, tiled=True)
    slots_here = received.shape[1]
    held = received.reshape(owners, local_experts, slots_here, model_width)
    pre_act = jnp.einsum("nlcd,ldh->nlch", held, w_in, preferred_element_type=jnp.float32)
    activation = jax.nn.gelu(pre_act).astype(jnp.bfloat16)
    expert_out = jnp.einsum(
        "nlch,lhd->nlcd", activation, w_out, preferred_element_type=jnp.float32
    ).astype(jnp.bfloat16)
    projected = jnp.einsum("nlcd,dk->nlck", expert_out, w_proj, preferred_element_type=jnp.float32)
    outcome = lax.all_to_all(
        projected.reshape(experts_all, slots_here, -1).astype(jnp.bfloat16),
        "expert",
        split_axis=0,
        concat_axis=0,
        tiled=True,
    ).astype(jnp.float32)
    flat_back = outcome.reshape(experts_all * capacity, -1)
    fetch = jnp.where(usable, slot_index, 0)
    picked = flat_back[fetch]
    weight_mix = jnp.where(usable, gates.reshape(-1), 0.0).reshape(tokens_dev, 2, 1)
    base_proj = jnp.dot(resident, w_proj, preferred_element_type=jnp.float32)
    slot_terms = picked.reshape(tokens_dev, 2, -1)
    neck_map = (base_proj + jnp.sum(slot_terms * weight_mix, axis=1)).astype(jnp.bfloat16)
    neck_map = neck_map.reshape(rows_dev, width_cols, -1)
    padded = padded_2(neck_map, (("slab", 0),), 1)
    hidden_core = jax.nn.gelu(conv_rows(padded, kernel_one)).astype(jnp.bfloat16)
    hidden = padded_2(hidden_core, (("slab", 0),), 1)
    joined = neck_map.astype(jnp.float32) + conv_rows(hidden, kernel_two)
    return joined.astype(jnp.bfloat16).reshape(maps_dev, rows_dev, width_cols, -1)


def solution(mesh):
    placed = (
        P("expert", "slab", None, None),
        P("expert", "slab", None, None),
        P("expert", "slab", None, None),
        P("expert", "slab", None, None),
        P("expert", None, None),
        P("expert", None, None),
        P(),
        P(),
        P(),
    )
    return jax.shard_map(
        shards,
        mesh=mesh,
        in_specs=placed,
        out_specs=P("expert", "slab", None, None),
        check_vma=False,
    )
```

profile of v0, /device:TPU:0, one launch (start us, length us, event | category | flops | bytes accessed | tf_op | source)
XLA Modules:
  0.0 190.2 jit_solution(8403136517008371936)
XLA Ops:
  0.0 0.8 broadcast_select_fusion
  1.2 0.7 multiply_add_fusion
  2.2 1.5 multiply_reduce_fusion
  3.8 1.5 multiply_convert_fusion
  5.3 1.1 broadcast_in_dim.20
  6.4 2.2 %reshape.240 = bf16[1024,1024]{1,0:T(8,128)(2,1)} reshape(bf16[512,2,1024]{2,1,0:T(2,128)(2,1)S(1)} %broadcast_in_dim.20) | data formatting | bytes 4194304 | tf_op jit(solution)/shard_map/reshape | solution.py:55
  8.6 8.0 %scatter_custom_fusion = bf16[1536,1024]{1,0:T(8,128)(2,1)} fusion(s32[1024]{0:T(1024)S(1)} %bitcast.91, bf16[1024,1024]{1,0:T(8,128)(2,1)} %reshape.240, bf16[]{:T(256)} %constant.11.clone.1), kind=kCustom, calls=%fused_computation.23 | custom fusion | bytes 3146240 | tf_op jit(solution)/shard_map/scatter | solution.py:59
  16.7 78.0 %all_to_all.10 = bf16[8,192,1024]{2,1,0:T(8,128)(2,1)} all-to-all(bf16[8,192,1024]{2,1,0:T(8,128)(2,1)} %bitcast.72), channel_id=1, replica_groups=mesh['slab'=4,'expert'=8] {'expert'}, dimensions={0} | all-to-all | bytes 6291456 | tf_op jit(solution)/shard_map/all_to_all | solution.py:62
  94.6 34.0 %fusion.8 = bf16[8,192,1024]{2,1,0:T(8,128)(2,1)} fusion(bf16[8,192,1024]{2,1,0:T(8,128)(2,1)} %all_to_all.10, bf16[1,4096,1024]{2,1,0:T(8,128)(2,1)} %param.14, bf16[1,1024,4096]{2,1,0:T(8,128)(2,1)} %param.13), kind=kOutput, calls=%fused_computation.11 | convolution fusion | flops 25826426880 | bytes 23068672 | tf_op jit(solution)/shard_map/nlch,lhd->nlcd/dot_general | solution.py:67
  128.6 3.8 %fusion.23 = bf16[8,192,256]{2,1,0:T(8,128)(2,1)} fusion(bf16[8,192,1024]{2,1,0:T(8,128)(2,1)} %fusion.8, bf16[1024,256]{1,0:T(8,128)(2,1)S(1)} %copy-done), kind=kOutput, calls=%fused_computation.25 | convolution fusion | flops 805699584 | bytes 4456448 | tf_op jit(solution)/shard_map/nlcd,dk->nlck/dot_general | solution.py:70
  132.4 3.8 %all-to-all-start.1 = ((bf16[8,192,256]{2,1,0:T(8,128)(2,1)}), bf16[8,192,256]{2,1,0:T(8,128)(2,1)S(1)}, u32[]{:S(2)}, u32[]{:S(2)}) async-start(bf16[8,192,256]{2,1,0:T(8,128)(2,1)} %fusion.23), calls=%async_computation.1 | async-start | bytes 1572864 | tf_op jit(solution)/shard_map/all_to_all | solution.py:71
  136.3 20.5 %all-to-all-done.1 = bf16[8,192,256]{2,1,0:T(8,128)(2,1)S(1)} async-done(((bf16[8,192,256]{2,1,0:T(8,128)(2,1)}), bf16[8,192,256]{2,1,0:T(8,128)(2,1)S(1)}, u32[]{:S(2)}, u32[]{:S(2)}) %all-to-all-start.1) | async-done | bytes 786464 | tf_op jit(solution)/shard_map/all_to_all | solution.py:71
  157.0 3.5 %gather_fusion = f32[1024,256]{1,0:T(8,128)S(1)} fusion(f32[1536,256]{1,0:T(8,128)S(1)} %bitcast_convert_fusion, s32[1024]{0:T(1024)S(1)} %broadcast_clamp_fusion), kind=kCustom, calls=%fused_computation | custom fusion | bytes 2101248 | tf_op jit(solution)/shard_map/gather | solution.py:80
  160.5 1.6 reshape.217
  162.1 4.0 %multiply_reduce_fusion.1 = f32[512,256]{1,0:T(8,128)S(1)} fusion(f32[512,2,256]{2,1,0:T(2,128)} %reshape.217, f32[512,2]{1,0:T(8,128)S(1)} %bitcast.89), kind=kLoop, calls=%fused_computation.36 | loop fusion | flops 393216 | bytes 1576960 | tf_op jit(solution)/shard_map/reduce_sum | solution.py:84
  166.1 0.4 fusion.27
  166.6 3.4 %collective-permute-start = (bf16[1,64,256]{2,1,0:T(8,128)(2,1)S(1)}, bf16[1,64,256]{2,1,0:T(8,128)(2,1)S(1)}, u32[]{:S(2)}, u32[]{:S(2)}) collective-permute-start(bf16[1,64,256]{2,1,0:T(8,128)(2,1)S(1)} %get-tuple-element.25), channel_id=1, source_target_pairs={{0,8},{8,16},{16,24},{1,9},{9,17},{17,25},{2,10},{10,18},{18,26},{... | collective-permute-start | bytes 98312 | tf_op jit(solution)/shard_map/ppermute | solution.py:12
  169.9 1.3 collective-permute-start.1
  171.5 4.2 %collective-permute-done.1 = bf16[1,64,256]{2,1,0:T(8,128)(2,1)S(1)} collective-permute-done((bf16[1,64,256]{2,1,0:T(8,128)(2,1)S(1)}, bf16[1,64,256]{2,1,0:T(8,128)(2,1)S(1)}, u32[]{:S(2)}, u32[]{:S(2)}) %collective-permute-start.1) | collective-permute-done | bytes 32800 | tf_op jit(solution)/shard_map/ppermute | solution.py:15
  177.7 4.3 %collective-permute-start.2 = (bf16[1,64,256]{2,1,0:T(8,128)(2,1)S(1)}, bf16[1,64,256]{2,1,0:T(8,128)(2,1)S(1)}, u32[]{:S(2)}, u32[]{:S(2)}) collective-permute-start(bf16[1,64,256]{2,1,0:T(8,128)(2,1)S(1)} %get-tuple-element.23), channel_id=1, source_target_pairs={{0,8},{8,16},{16,24},{1,9},{9,17},{17,25},{2,10},{10,18},{18,26},{... | collective-permute-start | bytes 98312 | tf_op jit(solution)/shard_map/ppermute | solution.py:12
  182.0 1.3 collective-permute-start.3
  183.6 4.2 %collective-permute-done.3 = bf16[1,64,256]{2,1,0:T(8,128)(2,1)S(1)} collective-permute-done((bf16[1,64,256]{2,1,0:T(8,128)(2,1)S(1)}, bf16[1,64,256]{2,1,0:T(8,128)(2,1)S(1)}, u32[]{:S(2)}, u32[]{:S(2)}) %collective-permute-start.3) | collective-permute-done | bytes 32800 | tf_op jit(solution)/shard_map/ppermute | solution.py:15
  188.7 0.4 convolution_add_fusion.1
  189.1 1.1 fusion.28
  (37 shorter events, 4.4 us)
Async XLA Ops:
  0.0 128.6 %copy-start = (bf16[1024,256]{1,0:T(8,128)(2,1)S(1)}, bf16[1024,256]{1,0:T(8,128)(2,1)}, u32[]{:S(2)}) copy-start(bf16[1024,256]{1,0:T(8,128)(2,1)} %param.15) | copy-start | bytes 1572868
  132.4 24.5 %all-to-all-start.1 = ((bf16[8,192,256]{2,1,0:T(8,128)(2,1)}), bf16[8,192,256]{2,1,0:T(8,128)(2,1)S(1)}, u32[]{:S(2)}, u32[]{:S(2)}) async-start(bf16[8,192,256]{2,1,0:T(8,128)(2,1)} %fusion.23), calls=%async_computation.1 | async-start | bytes 1572864 | tf_op jit(solution)/shard_map/all_to_all | solution.py:71
  160.5 5.6 %copy-start.1 = (bf16[1,8,64,1024]{3,2,1,0:T(8,128)(2,1)S(1)}, bf16[1,8,64,1024]{3,2,1,0:T(8,128)(2,1)}, u32[]{:S(2)}) copy-start(bf16[1,8,64,1024]{3,2,1,0:T(8,128)(2,1)} %param.9) | copy-start | bytes 3145732
  162.1 9.2 %copy-start.2 = (bf16[3,3,256,256]{3,2,1,0:T(8,128)(2,1)S(1)}, bf16[3,3,256,256]{3,2,1,0:T(8,128)(2,1)}, u32[]{:S(2)}) copy-start(bf16[3,3,256,256]{3,2,1,0:T(8,128)(2,1)} %param.16) | copy-start | bytes 3538948
  166.6 5.0 %collective-permute-start = (bf16[1,64,256]{2,1,0:T(8,128)(2,1)S(1)}, bf16[1,64,256]{2,1,0:T(8,128)(2,1)S(1)}, u32[]{:S(2)}, u32[]{:S(2)}) collective-permute-start(bf16[1,64,256]{2,1,0:T(8,128)(2,1)S(1)} %get-tuple-element.25), channel_id=1, source_target_pairs={{0,8},{8,16},{16,24},{1,9},{9,17},{17,25},{2,10},{10,18},{18,26},{... | collective-permute-start | bytes 98312 | tf_op jit(solution)/shard_map/ppermute | solution.py:12
  169.9 5.8 %collective-permute-start.1 = (bf16[1,64,256]{2,1,0:T(8,128)(2,1)S(1)}, bf16[1,64,256]{2,1,0:T(8,128)(2,1)S(1)}, u32[]{:S(2)}, u32[]{:S(2)}) collective-permute-start(bf16[1,64,256]{2,1,0:T(8,128)(2,1)S(1)} %get-tuple-element.26), channel_id=1, source_target_pairs={{8,0},{16,8},{24,16},{9,1},{17,9},{25,17},{10,2},{18,10},{26,18},{... | collective-permute-start | bytes 98312 | tf_op jit(solution)/shard_map/ppermute | solution.py:15
  176.3 7.0 %copy-start.3 = (bf16[3,3,256,256]{3,2,1,0:T(8,128)(2,1)S(1)}, bf16[3,3,256,256]{3,2,1,0:T(8,128)(2,1)}, u32[]{:S(2)}) copy-start(bf16[3,3,256,256]{3,2,1,0:T(8,128)(2,1)} %param.17) | copy-start | bytes 3538948
  177.7 5.9 %collective-permute-start.2 = (bf16[1,64,256]{2,1,0:T(8,128)(2,1)S(1)}, bf16[1,64,256]{2,1,0:T(8,128)(2,1)S(1)}, u32[]{:S(2)}, u32[]{:S(2)}) collective-permute-start(bf16[1,64,256]{2,1,0:T(8,128)(2,1)S(1)} %get-tuple-element.23), channel_id=1, source_target_pairs={{0,8},{8,16},{16,24},{1,9},{9,17},{17,25},{2,10},{10,18},{18,26},{... | collective-permute-start | bytes 98312 | tf_op jit(solution)/shard_map/ppermute | solution.py:12
  182.0 5.8 %collective-permute-start.3 = (bf16[1,64,256]{2,1,0:T(8,128)(2,1)S(1)}, bf16[1,64,256]{2,1,0:T(8,128)(2,1)S(1)}, u32[]{:S(2)}, u32[]{:S(2)}) collective-permute-start(bf16[1,64,256]{2,1,0:T(8,128)(2,1)S(1)} %get-tuple-element.24), channel_id=1, source_target_pairs={{8,0},{16,8},{24,16},{9,1},{17,9},{25,17},{10,2},{18,10},{26,18},{... | collective-permute-start | bytes 98312 | tf_op jit(solution)/shard_map/ppermute | solution.py:15
where the time goes:
time: 191 us; the launch traced here: 190 us
  blocking collectives  78 us (41%)
  matrix products  41.1 us (22%)
  waiting for transfers between devices  29.3 us (15%)
  local copies, waits for them, and re-layouts  18.2 us (10%)
  starting transfers between devices  14 us (7%)
  other arithmetic  9.17 us (5%)
    all_to_all x1, blocking collectives, shards(): lax.all_to_all(buffer, 'expert', split_axis=0, concat_axis=0, tiled=True)  78 us
    dot_general x1, matrix products, shards(): jnp.einsum('nlch,lhd->nlcd', activation, w_out, preferred_element_type=jn...  34 us
    all_to_all x1, waiting for transfers between devices, shards(): lax.all_to_all(projected.reshape(experts_all, slots_here, -1).astype(jnp....  20.5 us
    ppermute x2, waiting for transfers between devices, padded_2(): lax.ppermute(lax.slice_in_dim(block, 0, width, axis=dim), axis, backward)  8.46 us
    scatter x1, local copies, waits for them, and re-layouts, shards(): buffer = buffer.at[slot_index].set(token_rows, mode='drop').reshape(exper...  8.02 us
    ppermute x2, starting transfers between devices, padded_2(): lax.ppermute(lax.slice_in_dim(block, block.shape[dim] - width, None, axis...  7.69 us
    reduce_sum x1, other arithmetic, shards(): jnp.sum(slot_terms * weight_mix, axis=1)  3.98 us
  transfers between devices with their start and end apart: 5, of which 5 were waited for; matrix products, arithmetic and copies ran while one was open for 0% of the time, Pallas kernels for 0%

commit v1 on v0

v1 whole, which is shorter than its diff:
```python
import functools

import jax
import jax.numpy as jnp
from jax import lax
from jax.experimental import pallas as pl
from jax.experimental.pallas import tpu as pltpu
from jax.sharding import PartitionSpec as P

MESH = pl.DeviceIdType.MESH
HIDDEN_TILE = 1024
FUSE_TILE = 512


def gelu(value):
    inner = 0.7978845608028654 * (value + 0.044715 * (value * value * value))
    half = 0.5 * value
    return half + half * jnp.tanh(inner)


def paired(me, step, count):
    partner, bit = 0, 1
    while bit < count:
        partner = partner + ((me // bit + step // bit) % 2) * bit
        bit *= 2
    return partner


def kernel(
    owners, slabs, capacity, rows, cols,
    features, codes_row, codes_col, gates, w_in_hbm, w_out_hbm, w_proj_hbm, one_hbm, two_hbm,
    joined,
    w_in, w_out, w_proj, one, two, fused, normed, sent, held, back, returned, total,
    neck, hidden, columns,
    load_sem, sent_sem, held_sem, back_sem, returned_sem, edge_sent, edge_held,
):
    me = lax.axis_index("expert")
    slab = lax.axis_index("slab")
    tokens, width = features.shape
    hidden_units = w_in.shape[1]
    loads = [
        pltpu.make_async_copy(source, target, load_sem.at[place])
        for place, (source, target) in enumerate(
            [(w_out_hbm.at[0], w_out), (w_proj_hbm, w_proj), (w_in_hbm.at[0], w_in),
             (one_hbm, one), (two_hbm, two)]
        )
    ]
    for load in loads:
        load.start()

    barrier = pltpu.get_barrier_semaphore()

    @pl.loop(1, owners)
    def _(step):
        pl.semaphore_signal(
            barrier, inc=1, device_id=(slab, paired(me, step, owners)), device_id_type=MESH
        )

    @pl.when(slab > 0)
    def _():
        pl.semaphore_signal(barrier, inc=1, device_id=(slab - 1, me), device_id_type=MESH)

    @pl.when(slab < slabs - 1)
    def _():
        pl.semaphore_signal(barrier, inc=1, device_id=(slab + 1, me), device_id_type=MESH)

    @pl.loop(0, tokens // cols)
    def _(chunk):
        piece = pl.ds(pl.multiple_of(chunk * cols, cols), cols)
        wide = features[piece, :].astype(jnp.float32)
        scale = lax.rsqrt(jnp.mean(wide * wide, axis=1, keepdims=True) + 1e-06)
        normed[piece, :] = (wide * scale).astype(jnp.bfloat16)

    neighbours = jnp.minimum(slab, 1) + jnp.minimum(slabs - 1 - slab, 1)
    pl.semaphore_wait(barrier, owners - 1 + neighbours)

    def dispatch(step):
        return pltpu.make_async_remote_copy(
            src_ref=sent.at[step], dst_ref=held.at[step],
            send_sem=sent_sem.at[step], recv_sem=held_sem.at[step],
            device_id=(slab, paired(me, step, owners)), device_id_type=MESH,
        )

    def giveback(step):
        return pltpu.make_async_remote_copy(
            src_ref=back.at[step], dst_ref=returned.at[step],
            send_sem=back_sem.at[step], recv_sem=returned_sem.at[step],
            device_id=(slab, paired(me, step, owners)), device_id_type=MESH,
        )

    def packed(step):
        slot = paired(me, step, owners) * capacity + lax.broadcasted_iota(
            jnp.int32, (capacity, tokens), 0
        )
        chosen = (codes_row[0:1, :] == slot) | (codes_row[1:2, :] == slot)
        choice = jnp.where(chosen, 1.0, 0.0).astype(jnp.bfloat16)
        return jnp.dot(choice, normed[...], preferred_element_type=jnp.float32).astype(jnp.bfloat16)

    @pl.loop(0, owners - 1)
    def _(turn):
        step = owners - 1 - turn
        sent[step] = packed(step)
        dispatch(step).start()

    held[0] = packed(0)

    loads[0].wait()
    loads[1].wait()

    @pl.loop(0, hidden_units // FUSE_TILE)
    def _(tile):
        piece = pl.ds(pl.multiple_of(tile * FUSE_TILE, FUSE_TILE), FUSE_TILE)
        fused[piece, :] = jnp.dot(
            w_out[piece, :], w_proj[...], preferred_element_type=jnp.float32
        ).astype(jnp.bfloat16)

    total[...] = jnp.dot(features[...], w_proj[...], preferred_element_type=jnp.float32)
    loads[2].wait()

    def expert(step):
        block = held[step]
        result = jnp.zeros((capacity, fused.shape[1]), jnp.float32)
        for tile in range(hidden_units // HIDDEN_TILE):
            piece = slice(tile * HIDDEN_TILE, (tile + 1) * HIDDEN_TILE)
            pre = jnp.dot(block, w_in[:, piece], preferred_element_type=jnp.float32)
            result = result + jnp.dot(
                gelu(pre).astype(jnp.bfloat16), fused[piece, :], preferred_element_type=jnp.float32
            )
        back[step] = result.astype(jnp.bfloat16)

    def combine(step, source):
        slot = paired(me, step, owners) * capacity + lax.broadcasted_iota(
            jnp.int32, (tokens, capacity), 1
        )
        outcome = source[step]
        for choice in range(2):
            chosen = codes_col[:, choice : choice + 1] == slot
            picked = jnp.dot(
                jnp.where(chosen, 1.0, 0.0).astype(jnp.bfloat16), outcome,
                preferred_element_type=jnp.float32,
            )
            total[...] += gates[:, choice : choice + 1] * picked

    @pl.loop(0, owners)
    def _(turn):
        step = (owners - turn) % owners

        @pl.when(step > 0)
        def _():
            dispatch(step).wait_recv()

        expert(step)

        @pl.when(step > 0)
        def _():
            giveback(step).start()

    combine(0, back)

    @pl.loop(0, owners - 1)
    def _(turn):
        step = owners - 1 - turn
        giveback(step).wait_recv()
        combine(step, returned)

    loads[3].wait()
    loads[4].wait()
    inside = slice(cols, cols + tokens)

    def edges(place, field):
        up = pltpu.make_async_remote_copy(
            src_ref=field.at[pl.ds(cols, cols)], dst_ref=field.at[pl.ds(cols + tokens, cols)],
            send_sem=edge_sent.at[place, 0], recv_sem=edge_held.at[place, 0],
            device_id=(jnp.maximum(slab - 1, 0), me), device_id_type=MESH,
        )
        down = pltpu.make_async_remote_copy(
            src_ref=field.at[pl.ds(tokens, cols)], dst_ref=field.at[pl.ds(0, cols)],
            send_sem=edge_sent.at[place, 1], recv_sem=edge_held.at[place, 1],
            device_id=(jnp.minimum(slab + 1, slabs - 1), me), device_id_type=MESH,
        )
        return up, down

    def spread(field, piece, count):
        centre = field[piece, :]
        channels = centre.shape[1]
        wide = centre.astype(jnp.float32)
        column = lax.broadcasted_iota(jnp.int32, (count, 1), 0) % cols
        columns[piece, 0:channels] = jnp.where(
            column == 0, 0.0, pltpu.roll(wide, 1, 0)
        ).astype(jnp.bfloat16)
        columns[piece, channels : 2 * channels] = centre
        columns[piece, 2 * channels : 3 * channels] = jnp.where(
            column == cols - 1, 0.0, pltpu.roll(wide, count - 1, 0)
        ).astype(jnp.bfloat16)

    def convolved(place, field, taps):
        up, down = edges(place, field)

        @pl.when(slab > 0)
        def _():
            up.start()

        @pl.when(slab < slabs - 1)
        def _():
            down.start()

        @pl.when(slab == 0)
        def _():
            field[0:cols, :] = jnp.zeros((cols, field.shape[1]), jnp.bfloat16)

        @pl.when(slab == slabs - 1)
        def _():
            field[cols + tokens :, :] = jnp.zeros((cols, field.shape[1]), jnp.bfloat16)

        spread(field, inside, tokens)
        total[...] = jnp.dot(columns[inside, :], taps[1], preferred_element_type=jnp.float32)

        @pl.when(slab > 0)
        def _():
            down.wait_recv()

        @pl.when(slab < slabs - 1)
        def _():
            up.wait_recv()

        spread(field, slice(0, cols), cols)
        spread(field, slice(cols + tokens, 2 * cols + tokens), cols)
        return (
            total[...]
            + jnp.dot(columns[0:tokens, :], taps[0], preferred_element_type=jnp.float32)
            + jnp.dot(
                columns[2 * cols : 2 * cols + tokens, :], taps[2],
                preferred_element_type=jnp.float32,
            )
        )

    neck[inside, :] = total[...].astype(jnp.bfloat16)
    hidden[inside, :] = gelu(convolved(0, neck, one)).astype(jnp.bfloat16)
    joined[...] = (
        neck[inside, :].astype(jnp.float32) + convolved(1, hidden, two)
    ).astype(jnp.bfloat16)

    @pl.loop(1, owners)
    def _(step):
        dispatch(step).wait_send()
        giveback(step).wait_send()

    for place, field in enumerate((neck, hidden)):
        up, down = edges(place, field)

        @pl.when(slab > 0)
        def _():
            up.wait_send()

        @pl.when(slab < slabs - 1)
        def _():
            down.wait_send()


def shards(owners, slabs, features, expert_ids, positions, gates, w_in, w_out, w_proj, kernel_one,
           kernel_two):
    maps_dev, rows_dev, width_cols, model_width = features.shape
    tokens_dev = maps_dev * rows_dev * width_cols
    local_experts, _, hidden_units = w_in.shape
    capacity = 3 * tokens_dev // (owners * local_experts)
    channels = w_proj.shape[1]
    codes = jnp.where(positions < capacity, expert_ids * capacity + positions, -1)
    codes = codes.reshape(tokens_dev, 2)
    vmem = pl.BlockSpec(memory_space=pltpu.VMEM)
    anywhere = pl.BlockSpec(memory_space=pl.ANY)
    bf16, f32 = jnp.bfloat16, jnp.float32
    padded = tokens_dev + 2 * width_cols
    joined = pl.pallas_call(
        functools.partial(kernel, owners, slabs, capacity, rows_dev, width_cols),
        out_shape=jax.ShapeDtypeStruct((tokens_dev, channels), bf16),
        in_specs=[vmem] * 4 + [anywhere] * 5,
        out_specs=vmem,
        scratch_shapes=[
            pltpu.VMEM((model_width, hidden_units), bf16),
            pltpu.VMEM((hidden_units, model_width), bf16),
            pltpu.VMEM((model_width, channels), bf16),
            pltpu.VMEM((3, 3 * channels, channels), bf16),
            pltpu.VMEM((3, 3 * channels, channels), bf16),
            pltpu.VMEM((hidden_units, channels), bf16),
            pltpu.VMEM((tokens_dev, model_width), bf16),
            pltpu.VMEM((owners, capacity, model_width), bf16),
            pltpu.VMEM((owners, capacity, model_width), bf16),
            pltpu.VMEM((owners, capacity, channels), bf16),
            pltpu.VMEM((owners, capacity, channels), bf16),
            pltpu.VMEM((tokens_dev, channels), f32),
            pltpu.VMEM((padded, channels), bf16),
            pltpu.VMEM((padded, channels), bf16),
            pltpu.VMEM((padded, 3 * channels), bf16),
            pltpu.SemaphoreType.DMA((5,)),
            pltpu.SemaphoreType.DMA((owners,)),
            pltpu.SemaphoreType.DMA((owners,)),
            pltpu.SemaphoreType.DMA((owners,)),
            pltpu.SemaphoreType.DMA((owners,)),
            pltpu.SemaphoreType.DMA((2, 2)),
            pltpu.SemaphoreType.DMA((2, 2)),
        ],
        compiler_params=pltpu.CompilerParams(
            collective_id=0, has_side_effects=True, vmem_limit_bytes=56 * 2**20
        ),
    )(
        features.reshape(tokens_dev, model_width),
        codes.T,
        codes,
        gates.reshape(tokens_dev, 2),
        w_in,
        w_out,
        w_proj,
        kernel_one.reshape(3, 3 * channels, channels),
        kernel_two.reshape(3, 3 * channels, channels),
    )
    return joined.reshape(maps_dev, rows_dev, width_cols, channels)


def solution(mesh):
    placed = (
        P("expert", "slab", None, None),
        P("expert", "slab", None, None),
        P("expert", "slab", None, None),
        P("expert", "slab", None, None),
        P("expert", None, None),
        P("expert", None, None),
        P(),
        P(),
        P(),
    )
    return jax.shard_map(
        functools.partial(shards, mesh.shape["expert"], mesh.shape["slab"]),
        mesh=mesh,
        in_specs=placed,
        out_specs=P("expert", "slab", None, None),
        check_vma=False,
    )
```

time: 191 us -> 112 us (0.59)
  Pallas kernels: 0 us -> 107 us
  blocking collectives: 78 us -> 0 us
  matrix products: 41.1 us -> 0 us
  waiting for transfers between devices: 29.3 us -> 0 us
  local copies, waits for them, and re-layouts: 18.2 us -> 4.06 us
  starting transfers between devices: 14 us -> 0 us
  other arithmetic: 9.17 us -> 0.72 us
    pallas_call x0 -> x1, Pallas kernels: none -> 107 us  [shards(): pl.pallas_call(functools.partial(kernel, owners, slabs, capacity, rows_de...]
    all_to_all x1 -> x0, blocking collectives: 78 us -> none  [shards(): lax.all_to_all(buffer, 'expert', split_axis=0, concat_axis=0, tiled=True)]
    dot_general x9 -> x0, matrix products: 41.1 us -> none  [the longest x1 34 us: shards(): jnp.einsum('nlch,lhd->nlcd', activation, w_out, preferred_element_type=jn...]
    all_to_all x1 -> x0, waiting for transfers between devices: 20.5 us -> none  [shards(): lax.all_to_all(projected.reshape(experts_all, slots_here, -1).astype(jnp....]
    ppermute x4 -> x0, starting transfers between devices: 10.3 us -> none  [the longest x2 7.69 us: padded_2(): lax.ppermute(lax.slice_in_dim(block, block.shape[dim] - width, None, axis...]
    ppermute x4 -> x0, waiting for transfers between devices: 8.82 us -> none  [the longest x2 8.46 us: padded_2(): lax.ppermute(lax.slice_in_dim(block, 0, width, axis=dim), axis, backward)]
    scatter x1 -> x0, local copies, waits for them, and re-layouts: 8.02 us -> none  [shards(): buffer = buffer.at[slot_index].set(token_rows, mode='drop').reshape(exper...]
    reduce_sum x2 -> x0, other arithmetic: 5.49 us -> none  [the longest x1 3.98 us: shards(): jnp.sum(slot_terms * weight_mix, axis=1)]
  transfers between devices with their start and end apart: 5 -> 0, of which waited for: 5 -> 0; matrix products, arithmetic and copies ran while one was open for 0% -> 0% of each run, Pallas kernels for 0% -> 0%
where the time goes in v1:
time: 112 us
  Pallas kernels  107 us (96%)
  local copies, waits for them, and re-layouts  4.06 us (4%)
    pallas_call x1, Pallas kernels, shards(): pl.pallas_call(functools.partial(kernel, owners, slabs, capacity, rows_de...  107 us
    unnamed x4, local copies, waits for them, and re-layouts  3.22 us

profile of v1, /device:TPU:0, one launch (start us, length us, event | category | flops | bytes accessed | tf_op | source)
XLA Modules:
  0.0 111.8 jit_solution(7136182702400753717)
XLA Ops:
  0.0 0.7 compare_select_fusion
  0.7 0.1 copy.10
  0.9 0.0 copy-start
  0.9 0.7 copy.12.codes_row
  1.6 1.5 %copy.11 = f32[1,8,64,2]{3,2,1,0:T(8,128)} copy(f32[1,8,64,2]{2,3,1,0:T(2,128)} %param.12) | data formatting | bytes 8192 | tf_op args[3]
  3.1 0.0 copy-done
  3.1 107.0 %shard_map.91 = bf16[512,256]{1,0:T(8,128)(2,1)} custom-call(bf16[512,1024]{1,0:T(8,128)(2,1)} %bitcast.14, s32[2,512]{1,0:T(2,128)} %copy.12.codes_row, s32[512,2]{1,0:T(8,128)} %bitcast.9, f32[512,2]{1,0:T(8,128)} %bitcast.13, bf16[1,1024,4096]{2,1,0:T(8,128)(2,1)} %w_in_hbm.1, bf16[1,4096,1024]{2,1,0:T(8,128)(2,1)} %w_out_hbm.1, ...), custom_call_target="tpu_custom_call" | custom-call | tf_op jit(solution)/shard_map/pallas_call | solution.py:273
  110.1 1.7 %copy.14 = bf16[1,8,64,256]{3,2,1,0:T(8,128)(2,1)} copy(bf16[1,8,64,256]{3,2,1,0:T(8,128)(2,1)} %bitcast.12) | data formatting | bytes 524288
Async XLA Ops:
  0.9 2.3 %copy-start = (s32[1,8,64,2]{3,2,1,0:T(8,128)}, s32[1,8,64,2]{3,2,1,0:T(8,128)S(1)}, u32[]{:S(2)}) copy-start(s32[1,8,64,2]{3,2,1,0:T(8,128)S(1)} %copy.10) | copy-start | bytes 12292

commit v2 on v1

--- a/solution.py
+++ b/solution.py
@@ -114,7 +114,7 @@
             w_out[piece, :], w_proj[...], preferred_element_type=jnp.float32
         ).astype(jnp.bfloat16)
 
-    total[...] = jnp.dot(features[...], w_proj[...], preferred_element_type=jnp.float32)
+    total[0:tokens, :] = jnp.dot(features[...], w_proj[...], preferred_element_type=jnp.float32)
     loads[2].wait()
 
     def expert(step):
@@ -139,48 +139,56 @@
                 jnp.where(chosen, 1.0, 0.0).astype(jnp.bfloat16), outcome,
                 preferred_element_type=jnp.float32,
             )
-            total[...] += gates[:, choice : choice + 1] * picked
-
-    @pl.loop(0, owners)
-    def _(turn):
-        step = (owners - turn) % owners
-
-        @pl.when(step > 0)
-        def _():
-            dispatch(step).wait_recv()
-
+            total[0:tokens, :] += gates[:, choice : choice + 1] * picked
+
+    def serve(step):
+        dispatch(step).wait_recv()
         expert(step)
-
-        @pl.when(step > 0)
-        def _():
-            giveback(step).start()
-
-    combine(0, back)
-
-    @pl.loop(0, owners - 1)
-    def _(turn):
-        step = owners - 1 - turn
+        giveback(step).start()
+
+    def gather(step):
         giveback(step).wait_recv()
         combine(step, returned)
 
+    near = owners // 2
+    expert(0)
+
+    @pl.loop(1, near)
+    def _(step):
+        serve(step)
+
+    combine(0, back)
+
+    @pl.loop(1, near)
+    def _(step):
+        gather(step)
+
+    @pl.loop(0, owners - near)
+    def _(turn):
+        serve(owners - 1 - turn)
+
+    @pl.loop(0, owners - near)
+    def _(turn):
+        gather(owners - 1 - turn)
+
     loads[3].wait()
     loads[4].wait()
-    inside = slice(cols, cols + tokens)
-
-    def edges(place, field):
-        up = pltpu.make_async_remote_copy(
-            src_ref=field.at[pl.ds(cols, cols)], dst_ref=field.at[pl.ds(cols + tokens, cols)],
-            send_sem=edge_sent.at[place, 0], recv_sem=edge_held.at[place, 0],
-            device_id=(jnp.maximum(slab - 1, 0), me), device_id_type=MESH,
-        )
-        down = pltpu.make_async_remote_copy(
-            src_ref=field.at[pl.ds(tokens, cols)], dst_ref=field.at[pl.ds(0, cols)],
-            send_sem=edge_sent.at[place, 1], recv_sem=edge_held.at[place, 1],
-            device_id=(jnp.minimum(slab + 1, slabs - 1), me), device_id_type=MESH,
-        )
-        return up, down
-
-    def spread(field, piece, count):
+    halo = 2 * cols
+    end = halo + tokens
+    inside = slice(halo, end)
+    up = pltpu.make_async_remote_copy(
+        src_ref=neck.at[pl.ds(halo, halo)], dst_ref=neck.at[pl.ds(end, halo)],
+        send_sem=edge_sent.at[0], recv_sem=edge_held.at[0],
+        device_id=(jnp.maximum(slab - 1, 0), me), device_id_type=MESH,
+    )
+    down = pltpu.make_async_remote_copy(
+        src_ref=neck.at[pl.ds(tokens, halo)], dst_ref=neck.at[pl.ds(0, halo)],
+        send_sem=edge_sent.at[1], recv_sem=edge_held.at[1],
+        device_id=(jnp.minimum(slab + 1, slabs - 1), me), device_id_type=MESH,
+    )
+
+    def spread(field, start, count):
+        piece = slice(start, start + count)
         centre = field[piece, :]
         channels = centre.shape[1]
         wide = centre.astype(jnp.float32)
@@ -193,51 +201,65 @@
             column == cols - 1, 0.0, pltpu.roll(wide, count - 1, 0)
         ).astype(jnp.bfloat16)
 
-    def convolved(place, field, taps):
-        up, down = edges(place, field)
-
-        @pl.when(slab > 0)
-        def _():
-            up.start()
-
-        @pl.when(slab < slabs - 1)
-        def _():
-            down.start()
-
-        @pl.when(slab == 0)
-        def _():
-            field[0:cols, :] = jnp.zeros((cols, field.shape[1]), jnp.bfloat16)
-
-        @pl.when(slab == slabs - 1)
-        def _():
-            field[cols + tokens :, :] = jnp.zeros((cols, field.shape[1]), jnp.bfloat16)
-
-        spread(field, inside, tokens)
-        total[...] = jnp.dot(columns[inside, :], taps[1], preferred_element_type=jnp.float32)
-
-        @pl.when(slab > 0)
-        def _():
-            down.wait_recv()
-
-        @pl.when(slab < slabs - 1)
-        def _():
-            up.wait_recv()
-
-        spread(field, slice(0, cols), cols)
-        spread(field, slice(cols + tokens, 2 * cols + tokens), cols)
-        return (
-            total[...]
-            + jnp.dot(columns[0:tokens, :], taps[0], preferred_element_type=jnp.float32)
-            + jnp.dot(
-                columns[2 * cols : 2 * cols + tokens, :], taps[2],
-                preferred_element_type=jnp.float32,
-            )
-        )
-
-    neck[inside, :] = total[...].astype(jnp.bfloat16)
-    hidden[inside, :] = gelu(convolved(0, neck, one)).astype(jnp.bfloat16)
+    def tapped(taps, row, start, count):
+        return jnp.dot(
+            columns[start : start + count, :], taps[row], preferred_element_type=jnp.float32
+        )
+
+    neck[inside, :] = total[0:tokens, :].astype(jnp.bfloat16)
+
+    @pl.when(slab > 0)
+    def _():
+        up.start()
+
+    @pl.when(slab < slabs - 1)
+    def _():
+        down.start()
+
+    @pl.when(slab == 0)
+    def _():
+        neck[0:halo, :] = jnp.zeros((halo, neck.shape[1]), jnp.bfloat16)
+
+    @pl.when(slab == slabs - 1)
+    def _():
+        neck[end : end + halo, :] = jnp.zeros((halo, neck.shape[1]), jnp.bfloat16)
+
+    spread(neck, halo, tokens)
+    total[0:tokens, :] = tapped(one, 2, halo, tokens)
+    total[tokens:end, :] = jnp.zeros((halo, total.shape[1]), jnp.float32)
+    total[cols : cols + tokens, :] += tapped(one, 1, halo, tokens)
+    total[halo:end, :] += tapped(one, 0, halo, tokens)
+
+    @pl.when(slab > 0)
+    def _():
+        down.wait_recv()
+
+    @pl.when(slab < slabs - 1)
+    def _():
+        up.wait_recv()
+
+    spread(neck, 0, halo)
+    spread(neck, end, halo)
+    total[0:halo, :] += tapped(one, 0, 0, halo)
+    total[0:cols, :] += tapped(one, 1, cols, cols)
+    total[tokens:end, :] += tapped(one, 2, end, halo)
+    total[end - cols : end, :] += tapped(one, 1, end, cols)
+    hidden[...] = gelu(total[...]).astype(jnp.bfloat16)
+
+    @pl.when(slab == 0)
+    def _():
+        hidden[0:cols, :] = jnp.zeros((cols, hidden.shape[1]), jnp.bfloat16)
+
+    @pl.when(slab == slabs - 1)
+    def _():
+        hidden[end - cols : end, :] = jnp.zeros((cols, hidden.shape[1]), jnp.bfloat16)
+
+    spread(hidden, 0, end)
     joined[...] = (
-        neck[inside, :].astype(jnp.float32) + convolved(1, hidden, two)
+        neck[inside, :].astype(jnp.float32)
+        + tapped(two, 0, 0, tokens)
+        + tapped(two, 1, cols, tokens)
+        + tapped(two, 2, halo, tokens)
     ).astype(jnp.bfloat16)
 
     @pl.loop(1, owners)
@@ -245,16 +267,13 @@
         dispatch(step).wait_send()
         giveback(step).wait_send()
 
-    for place, field in enumerate((neck, hidden)):
-        up, down = edges(place, field)
-
-        @pl.when(slab > 0)
-        def _():
-            up.wait_send()
-
-        @pl.when(slab < slabs - 1)
-        def _():
-            down.wait_send()
+    @pl.when(slab > 0)
+    def _():
+        up.wait_send()
+
+    @pl.when(slab < slabs - 1)
+    def _():
+        down.wait_send()
 
 
 def shards(owners, slabs, features, expert_ids, positions, gates, w_in, w_out, w_proj, kernel_one,
@@ -287,17 +306,17 @@
             pltpu.VMEM((owners, capacity, model_width), bf16),
             pltpu.VMEM((owners, capacity, channels), bf16),
             pltpu.VMEM((owners, capacity, channels), bf16),
-            pltpu.VMEM((tokens_dev, channels), f32),
+            pltpu.VMEM((padded, channels), f32),
+            pltpu.VMEM((padded + 2 * width_cols, channels), bf16),
             pltpu.VMEM((padded, channels), bf16),
-            pltpu.VMEM((padded, channels), bf16),
-            pltpu.VMEM((padded, 3 * channels), bf16),
+            pltpu.VMEM((padded + 2 * width_cols, 3 * channels), bf16),
             pltpu.SemaphoreType.DMA((5,)),
             pltpu.SemaphoreType.DMA((owners,)),
             pltpu.SemaphoreType.DMA((owners,)),
             pltpu.SemaphoreType.DMA((owners,)),
             pltpu.SemaphoreType.DMA((owners,)),
-            pltpu.SemaphoreType.DMA((2, 2)),
-            pltpu.SemaphoreType.DMA((2, 2)),
+            pltpu.SemaphoreType.DMA((2,)),
+            pltpu.SemaphoreType.DMA((2,)),
         ],
         compiler_params=pltpu.CompilerParams(
             collective_id=0, has_side_effects=True, vmem_limit_bytes=56 * 2**20

time: 112 us -> 108 us (0.964)
  the two profiles are of different devices: /device:TPU:0 before, /device:TPU:12 now
where the time goes in v2:
time: 108 us
  Pallas kernels  103 us (95%)
  local copies, waits for them, and re-layouts  4.06 us (4%)
    pallas_call x1, Pallas kernels, shards(): pl.pallas_call(functools.partial(kernel, owners, slabs, capacity, rows_de...  103 us
    unnamed x4, local copies, waits for them, and re-layouts  3.22 us

profile of v2, /device:TPU:12, one launch (start us, length us, event | category | flops | bytes accessed | tf_op | source)
XLA Modules:
  0.0 108.0 jit_solution(11048473557204724699)
XLA Ops:
  0.0 0.7 compare_select_fusion
  0.7 0.1 copy.10
  0.9 0.0 copy-start
  0.9 0.7 copy.12.codes_row
  1.6 1.5 %copy.11 = f32[1,8,64,2]{3,2,1,0:T(8,128)} copy(f32[1,8,64,2]{2,3,1,0:T(2,128)} %param.12) | data formatting | bytes 8192 | tf_op args[3]
  3.1 0.0 copy-done
  3.1 103.2 %shard_map.91 = bf16[512,256]{1,0:T(8,128)(2,1)} custom-call(bf16[512,1024]{1,0:T(8,128)(2,1)} %bitcast.14, s32[2,512]{1,0:T(2,128)} %copy.12.codes_row, s32[512,2]{1,0:T(8,128)} %bitcast.9, f32[512,2]{1,0:T(8,128)} %bitcast.13, bf16[1,1024,4096]{2,1,0:T(8,128)(2,1)} %w_in_hbm.1, bf16[1,4096,1024]{2,1,0:T(8,128)(2,1)} %w_out_hbm.1, ...), custom_call_target="tpu_custom_call" | custom-call | tf_op jit(solution)/shard_map/pallas_call | solution.py:292
  106.3 1.7 %copy.14 = bf16[1,8,64,256]{3,2,1,0:T(8,128)(2,1)} copy(bf16[1,8,64,256]{3,2,1,0:T(8,128)(2,1)} %bitcast.12) | data formatting | bytes 524288
Async XLA Ops:
  0.9 2.3 %copy-start = (s32[1,8,64,2]{3,2,1,0:T(8,128)}, s32[1,8,64,2]{3,2,1,0:T(8,128)S(1)}, u32[]{:S(2)}) copy-start(s32[1,8,64,2]{3,2,1,0:T(8,128)S(1)} %copy.10) | copy-start | bytes 12292

commit v3 on v2

--- a/solution.py
+++ b/solution.py
@@ -28,7 +28,7 @@
 
 def kernel(
     owners, slabs, capacity, rows, cols,
-    features, codes_row, codes_col, gates, w_in_hbm, w_out_hbm, w_proj_hbm, one_hbm, two_hbm,
+    features, codes_row, gates, w_in_hbm, w_out_hbm, w_proj_hbm, one_hbm, two_hbm,
     joined,
     w_in, w_out, w_proj, one, two, fused, normed, sent, held, back, returned, total,
     neck, hidden, columns,
@@ -130,16 +130,18 @@
 
     def combine(step, source):
         slot = paired(me, step, owners) * capacity + lax.broadcasted_iota(
-            jnp.int32, (tokens, capacity), 1
-        )
+            jnp.int32, (capacity, tokens), 0
+        )
+        weight = jnp.where(codes_row[0:1, :] == slot, gates[0:1, :], 0.0) + jnp.where(
+            codes_row[1:2, :] == slot, gates[1:2, :], 0.0
+        )
+        coarse = weight.astype(jnp.bfloat16)
+        fine = (weight - coarse.astype(jnp.float32)).astype(jnp.bfloat16)
         outcome = source[step]
-        for choice in range(2):
-            chosen = codes_col[:, choice : choice + 1] == slot
-            picked = jnp.dot(
-                jnp.where(chosen, 1.0, 0.0).astype(jnp.bfloat16), outcome,
-                preferred_element_type=jnp.float32,
+        for part in (coarse, fine):
+            total[0:tokens, :] += lax.dot_general(
+                part, outcome, (((0,), (0,)), ((), ())), preferred_element_type=jnp.float32
             )
-            total[0:tokens, :] += gates[:, choice : choice + 1] * picked
 
     def serve(step):
         dispatch(step).wait_recv()
@@ -284,7 +286,7 @@
     capacity = 3 * tokens_dev // (owners * local_experts)
     channels = w_proj.shape[1]
     codes = jnp.where(positions < capacity, expert_ids * capacity + positions, -1)
-    codes = codes.reshape(tokens_dev, 2)
+    codes = codes.reshape(tokens_dev, 2).T
     vmem = pl.BlockSpec(memory_space=pltpu.VMEM)
     anywhere = pl.BlockSpec(memory_space=pl.ANY)
     bf16, f32 = jnp.bfloat16, jnp.float32
@@ -292,7 +294,7 @@
     joined = pl.pallas_call(
         functools.partial(kernel, owners, slabs, capacity, rows_dev, width_cols),
         out_shape=jax.ShapeDtypeStruct((tokens_dev, channels), bf16),
-        in_specs=[vmem] * 4 + [anywhere] * 5,
+        in_specs=[vmem] * 3 + [anywhere] * 5,
         out_specs=vmem,
         scratch_shapes=[
             pltpu.VMEM((model_width, hidden_units), bf16),
@@ -323,9 +325,8 @@
         ),
     )(
         features.reshape(tokens_dev, model_width),
-        codes.T,
         codes,
-        gates.reshape(tokens_dev, 2),
+        gates.reshape(tokens_dev, 2).T,
         w_in,
         w_out,
         w_proj,

time: 108 us -> 108 us (level)
    reshape x0 -> x2, local copies, waits for them, and re-layouts: none -> 1.34 us  [the longest x1 0.67 us: shards(): codes = codes.reshape(tokens_dev, 2).T]
    unnamed x4 -> x2, local copies, waits for them, and re-layouts: 3.22 us -> 2.37 us
where the time goes in v3:
time: 108 us; the launch traced here: 107 us
  Pallas kernels  103 us (95%)
  local copies, waits for them, and re-layouts  3.71 us (3%)
    pallas_call x1, Pallas kernels, shards(): pl.pallas_call(functools.partial(kernel, owners, slabs, capacity, rows_de...  103 us
    unnamed x2, local copies, waits for them, and re-layouts  2.37 us

profile of v3, /device:TPU:12, one launch (start us, length us, event | category | flops | bytes accessed | tf_op | source)
XLA Modules:
  0.0 107.3 jit_solution(8387537671998218108)
XLA Ops:
  0.0 0.7 compare_select_fusion
  0.7 0.7 reshape.19
  1.4 0.7 copy.11
  2.1 0.7 reshape.20
  2.8 102.8 %shard_map.91 = bf16[512,256]{1,0:T(8,128)(2,1)} custom-call(bf16[512,1024]{1,0:T(8,128)(2,1)} %bitcast.17, s32[2,512]{1,0:T(2,128)} %bitcast.18, f32[2,512]{1,0:T(2,128)} %bitcast.19, bf16[1,1024,4096]{2,1,0:T(8,128)(2,1)} %w_in_hbm.1, bf16[1,4096,1024]{2,1,0:T(8,128)(2,1)} %w_out_hbm.1, bf16[1024,256]{1,0:T(8,128)(2,1)} %w_proj_hbm.1, ...), custom_call_target="tpu_custom_call" | custom-call | tf_op jit(solution)/shard_map/pallas_call | solution.py:294
  105.6 1.7 %copy.13 = bf16[1,8,64,256]{3,2,1,0:T(8,128)(2,1)} copy(bf16[1,8,64,256]{3,2,1,0:T(8,128)(2,1)} %bitcast.16) | data formatting | bytes 524288
  (1 shorter events, 0.0 us)

commit v4 on v3

--- a/solution.py
+++ b/solution.py
@@ -152,24 +152,14 @@
         giveback(step).wait_recv()
         combine(step, returned)
 
-    near = owners // 2
     expert(0)
-
-    @pl.loop(1, near)
-    def _(step):
-        serve(step)
-
     combine(0, back)
 
-    @pl.loop(1, near)
-    def _(step):
-        gather(step)
-
-    @pl.loop(0, owners - near)
+    @pl.loop(0, owners - 1)
     def _(turn):
         serve(owners - 1 - turn)
 
-    @pl.loop(0, owners - near)
+    @pl.loop(0, owners - 1)
     def _(turn):
         gather(owners - 1 - turn)
 

time: 108 us -> 108 us (level)
  the two profiles are of different devices: /device:TPU:12 before, /device:TPU:0 now
where the time goes in v4:
time: 108 us; the launch traced here: 107 us
  Pallas kernels  103 us (95%)
  local copies, waits for them, and re-layouts  3.71 us (3%)
    pallas_call x1, Pallas kernels, shards(): pl.pallas_call(functools.partial(kernel, owners, slabs, capacity, rows_de...  103 us
    unnamed x2, local copies, waits for them, and re-layouts  2.37 us

profile of v4, /device:TPU:0, one launch (start us, length us, event | category | flops | bytes accessed | tf_op | source)
XLA Modules:
  0.0 107.2 jit_solution(11339797506630844991)
XLA Ops:
  0.0 0.7 compare_select_fusion
  0.7 0.7 reshape.19
  1.4 0.7 copy.11
  2.1 0.7 reshape.20
  2.8 102.8 %shard_map.91 = bf16[512,256]{1,0:T(8,128)(2,1)} custom-call(bf16[512,1024]{1,0:T(8,128)(2,1)} %bitcast.17, s32[2,512]{1,0:T(2,128)} %bitcast.18, f32[2,512]{1,0:T(2,128)} %bitcast.19, bf16[1,1024,4096]{2,1,0:T(8,128)(2,1)} %w_in_hbm.1, bf16[1,4096,1024]{2,1,0:T(8,128)(2,1)} %w_out_hbm.1, bf16[1024,256]{1,0:T(8,128)(2,1)} %w_proj_hbm.1, ...), custom_call_target="tpu_custom_call" | custom-call | tf_op jit(solution)/shard_map/pallas_call | solution.py:284
  105.6 1.7 %copy.13 = bf16[1,8,64,256]{3,2,1,0:T(8,128)(2,1)} copy(bf16[1,8,64,256]{3,2,1,0:T(8,128)(2,1)} %bitcast.16) | data formatting | bytes 524288
  (1 shorter events, 0.0 us)
